TPU v7x, 32 devices: a whole 2x2x4 slice. The times are simulated.
32 devices in a mesh: groups: 2 (over x), ctx: 16 (over z, y, core).
Axes of the slice: x: 2, y: 2, z: 4, core: 2. Of those that a mesh axis runs over, the one named last changes fastest.
Arguments:
- queries: bfloat16 [6144, 4096], P(('groups', 'ctx')), parts along dimension 0, may hold values from -6 to 6
- keys: bfloat16 [6144, 1024], P(('groups', 'ctx')), parts along dimension 0, may hold values from -6 to 6
- values: bfloat16 [6144, 1024], P(('groups', 'ctx')), parts along dimension 0, may hold values from -6 to 6
- grad_out: bfloat16 [6144, 4096], P(('groups', 'ctx')), parts along dimension 0, may hold values from -6 to 6
- positions: int32 [6144], P('groups'), parts along dimension 0, may hold values from 0 to 3071, as said below
- segments: int32 [6144], P('groups'), parts along dimension 0, may hold values from 0 to 1, as said below
Outputs:
- grad_queries: bfloat16 [6144, 4096], P(('groups', 'ctx')), parts along dimension 0
- grad_keys: bfloat16 [6144, 1024], P(('groups', 'ctx')), parts along dimension 0
- grad_values: bfloat16 [6144, 1024], P(('groups', 'ctx')), parts along dimension 0
There are 2 independent parts, one for each index of `groups`. A program takes and returns all parts, laid end to end along the dimension named above; each array names one. Nothing has to cross between parts.
Inputs may be any that keep to these rules, and one draw needn't show every extreme that they name: Rows b * 192 to (b + 1) * 192 - 1 hold the positions b * 192 to (b + 1) * 192 - 1, each once, in some order. `segments`: document ids never fall as positions rise; two tokens are in the same document exactly when their ids are equal. Each aligned run of 1536 positions holds exactly one document start, the first at position 0.
All inputs are finite; a program needn't handle non-finite values.
Results may differ from a plain program's by a relative error of at most 0.0087.
Values may be sent and summed in bfloat16 or wider, within the bound.
A program may use at most 128 MiB of HBM per device.

v0:
```python
import functools

import jax
import jax.numpy as jnp
from jax import lax
from jax.experimental import pallas as pl
from jax.experimental.pallas import tpu as pltpu
from jax.sharding import PartitionSpec as P

HQ = 32
HK = 8
DH = 128
GROUP = HQ // HK
WINDOW = 768
HALO = 4
SCALE = float(DH) ** (-0.5)
LOG2E = 1.4426950408889634
NEG = -1e30
NT = (((1,), (1,)), ((), ()))
TN = (((0,), (0,)), ((), ()))
NN = (((1,), (0,)), ((), ()))


def dot(a, b, dims):
    return lax.dot_general(a, b, dims, preferred_element_type=jnp.float32)


def tile_grads(k, v, q, do, bias):
    s = dot(k, q, NT) + bias
    dp = dot(v, do, NT)
    m = jnp.max(s, axis=0, keepdims=True)
    e = jnp.exp2((s - m) * (SCALE * LOG2E))
    inv = 1.0 / jnp.sum(e, axis=0, keepdims=True)
    delta = jnp.sum(e * dp, axis=0, keepdims=True) * inv
    p = (e * inv).astype(jnp.bfloat16)
    a = inv * SCALE
    ds = (e * (dp * a - delta * a)).astype(jnp.bfloat16)
    dv = dot(p, do, NN)
    dk = dot(ds, q, NN)
    dq = dot(ds, k, TN)
    return dq, dk, dv


CHUNK = 256


def kernel(q_ref, do_ref, k_ref, v_ref, bias_ref, dq_ref, dk_ref, dv_ref, bias4):
    tok = q_ref.shape[0]

    @pl.when(pl.program_id(0) == 0)
    def _():
        b = bias_ref[...]
        bias4[...] = jnp.concatenate([b] * GROUP, axis=1)

    k = k_ref[...]
    v = v_ref[...]
    q = jnp.concatenate([q_ref[:, g * DH:(g + 1) * DH] for g in range(GROUP)], axis=0)
    do = jnp.concatenate([do_ref[:, g * DH:(g + 1) * DH] for g in range(GROUP)], axis=0)
    dqs = []
    dk = dv = None
    for c in range(GROUP * tok // CHUNK):
        cut = slice(c * CHUNK, (c + 1) * CHUNK)
        dq, dk1, dv1 = tile_grads(k, v, q[cut], do[cut], bias4[:, cut])
        dqs.append(dq.astype(jnp.bfloat16))
        dk = dk1 if dk is None else dk + dk1
        dv = dv1 if dv is None else dv + dv1
    dq = jnp.concatenate(dqs, axis=0)
    for g in range(GROUP):
        dq_ref[:, g * DH:(g + 1) * DH] = dq[g * tok:(g + 1) * tok]
    dk_ref[...] = dk.astype(jnp.bfloat16)
    dv_ref[...] = dv.astype(jnp.bfloat16)


def shift(x, distance):
    n = lax.axis_size("ctx")
    route = [(i, i + distance) for i in range(n) if 0 <= i + distance < n]
    return lax.ppermute(x, "ctx", route)


def per_device(queries, keys, values, grad_out, positions, segments):
    tok = queries.shape[0]
    me = lax.axis_index("ctx")
    span = (HALO + 1) * tok
    kv = jnp.concatenate([keys, values], axis=1)
    kv_all = jnp.concatenate([shift(kv, d) for d in range(HALO, 0, -1)] + [kv], axis=0)
    pos_pad = jnp.concatenate([jnp.full((HALO * tok,), -1, jnp.int32), positions])
    seg_pad = jnp.concatenate([jnp.full((HALO * tok,), -1, jnp.int32), segments])
    kpos = lax.dynamic_slice_in_dim(pos_pad, me * tok, span)[:, None]
    kseg = lax.dynamic_slice_in_dim(seg_pad, me * tok, span)[:, None]
    qpos = lax.dynamic_slice_in_dim(positions, me * tok, tok)[None, :]
    qseg = lax.dynamic_slice_in_dim(segments, me * tok, tok)[None, :]
    mask = (kseg == qseg) & (kpos <= qpos) & (qpos - kpos < WINDOW)
    bias = jnp.where(mask, 0.0, NEG).astype(jnp.float32)
    kd = HK * DH
    dq, dk, dv = pl.pallas_call(
        kernel,
        grid=(HK,),
        in_specs=[
            pl.BlockSpec((tok, GROUP * DH), lambda h: (0, h)),
            pl.BlockSpec((tok, GROUP * DH), lambda h: (0, h)),
            pl.BlockSpec((span, DH), lambda h: (0, h)),
            pl.BlockSpec((span, DH), lambda h: (0, h + HK)),
            pl.BlockSpec((span, tok), lambda h: (0, 0)),
        ],
        out_specs=[
            pl.BlockSpec((tok, GROUP * DH), lambda h: (0, h)),
            pl.BlockSpec((span, DH), lambda h: (0, h)),
            pl.BlockSpec((span, DH), lambda h: (0, h)),
        ],
        out_shape=[
            jax.ShapeDtypeStruct((tok, HQ * DH), jnp.bfloat16),
            jax.ShapeDtypeStruct((span, kd), jnp.bfloat16),
            jax.ShapeDtypeStruct((span, kd), jnp.bfloat16),
        ],
        scratch_shapes=[pltpu.VMEM((span, GROUP * tok), jnp.float32)],
        compiler_params=pltpu.CompilerParams(vmem_limit_bytes=48 * 1024 * 1024),
    )(queries, grad_out, kv_all, kv_all, bias)
    own = jnp.stack([dk[HALO * tok:], dv[HALO * tok:]]).astype(jnp.float32)
    for d in range(1, HALO + 1):
        lo = (HALO - d) * tok
        part = jnp.stack([dk[lo:lo + tok], dv[lo:lo + tok]])
        own = own + shift(part, -d).astype(jnp.float32)
    own = own.astype(jnp.bfloat16)
    return dq, own[0], own[1]


def solution(mesh):
    rows = P(("groups", "ctx"), None)
    return jax.shard_map(
        per_device,
        mesh=mesh,
        in_specs=(rows, rows, rows, rows, P("groups"), P("groups")),
        out_specs=(rows, rows, rows),
        check_vma=False,
    )
```

profile of v0, /device:TPU:0, one launch (start us, length us, event | category | flops | bytes accessed | tf_op | source)
XLA Modules:
  0.0 172.7 jit_solution(677107150910076351)
XLA Ops:
  0.6 1.8 %constant_dynamic-update-slice_fusion.1 = bf16[192,2048]{1,0:T(8,128)(2,1)} fusion(bf16[192,1024]{1,0:T(8,128)(2,1)} %param.7), kind=kLoop, calls=%fused_computation.21 | loop fusion | bytes 786432
  2.4 1.8 %constant_dynamic-update-slice_fusion = bf16[192,2048]{1,0:T(8,128)(2,1)} fusion(bf16[192,2048]{1,0:T(8,128)(2,1)} %constant_dynamic-update-slice_fusion.1, bf16[192,1024]{1,0:T(8,128)(2,1)} %param.8), kind=kLoop, calls=%fused_computation.20 | loop fusion | bytes 786432 | tf_op jit(solution)/shard_map/concatenate | solution.py:84
  4.2 5.0 %collective-permute-start = (bf16[192,2048]{1,0:T(8,128)(2,1)}, bf16[192,2048]{1,0:T(8,128)(2,1)S(1)}, u32[]{:S(2)}, u32[]{:S(2)}) collective-permute-start(bf16[192,2048]{1,0:T(8,128)(2,1)} %constant_dynamic-update-slice_fusion), channel_id=1, source_target_pairs={{0,4},{1,5},{2,6},{3,7},{4,8},{5,9},{6,10},{7,11},{8,12},{9,13},{1... | collective-permute-start | bytes 2359304 | tf_op jit(solution)/shard_map/ppermute | solution.py:77
  9.2 2.6 %collective-permute-start.1 = (bf16[192,2048]{1,0:T(8,128)(2,1)}, bf16[192,2048]{1,0:T(8,128)(2,1)S(1)}, u32[]{:S(2)}, u32[]{:S(2)}) collective-permute-start(bf16[192,2048]{1,0:T(8,128)(2,1)} %constant_dynamic-update-slice_fusion), channel_id=1, source_target_pairs={{0,3},{1,4},{2,5},{3,6},{4,7},{5,8},{6,9},{7,10},{8,11},{9,12},{10... | collective-permute-start | bytes 2359304 | tf_op jit(solution)/shard_map/ppermute | solution.py:77
  11.8 3.4 %collective-permute-start.2 = (bf16[192,2048]{1,0:T(8,128)(2,1)}, bf16[192,2048]{1,0:T(8,128)(2,1)S(1)}, u32[]{:S(2)}, u32[]{:S(2)}) collective-permute-start(bf16[192,2048]{1,0:T(8,128)(2,1)} %constant_dynamic-update-slice_fusion), channel_id=1, source_target_pairs={{0,2},{1,3},{2,4},{3,5},{4,6},{5,7},{6,8},{7,9},{8,10},{9,11},{10,... | collective-permute-start | bytes 2359304 | tf_op jit(solution)/shard_map/ppermute | solution.py:77
  15.3 2.6 %collective-permute-start.3 = (bf16[192,2048]{1,0:T(8,128)(2,1)}, bf16[192,2048]{1,0:T(8,128)(2,1)S(1)}, u32[]{:S(2)}, u32[]{:S(2)}) collective-permute-start(bf16[192,2048]{1,0:T(8,128)(2,1)} %constant_dynamic-update-slice_fusion), channel_id=1, source_target_pairs={{0,1},{1,2},{2,3},{3,4},{4,5},{5,6},{6,7},{7,8},{8,9},{9,10},{10,1... | collective-permute-start | bytes 2359304 | tf_op jit(solution)/shard_map/ppermute | solution.py:77
  17.9 0.8 pad_dynamic-slice_fusion
  18.7 0.8 dynamic_slice.13
  19.5 0.8 dynamic_slice.15
  20.3 0.3 fusion.1.bias_ref
  20.6 6.8 %collective-permute-done = bf16[192,2048]{1,0:T(8,128)(2,1)S(1)} collective-permute-done((bf16[192,2048]{1,0:T(8,128)(2,1)}, bf16[192,2048]{1,0:T(8,128)(2,1)S(1)}, u32[]{:S(2)}, u32[]{:S(2)}) %collective-permute-start) | collective-permute-done | bytes 786464 | tf_op jit(solution)/shard_map/ppermute | solution.py:77
  27.5 0.1 constant_dynamic-update-slice_fusion.5
  27.5 15.9 %collective-permute-done.2 = bf16[192,2048]{1,0:T(8,128)(2,1)S(1)} collective-permute-done((bf16[192,2048]{1,0:T(8,128)(2,1)}, bf16[192,2048]{1,0:T(8,128)(2,1)S(1)}, u32[]{:S(2)}, u32[]{:S(2)}) %collective-permute-start.2) | collective-permute-done | bytes 786464 | tf_op jit(solution)/shard_map/ppermute | solution.py:77
  43.6 1.8 %copy-done.2 = bf16[960,2048]{1,0:T(8,128)(2,1)} copy-done((bf16[960,2048]{1,0:T(8,128)(2,1)}, bf16[960,2048]{1,0:T(8,128)(2,1)S(1)}, u32[]{:S(2)}) %copy-start.2) | copy-done | bytes 3932184
  45.4 33.0 %shard_map.85 = (bf16[192,4096]{1,0:T(8,128)(2,1)}, bf16[960,1024]{1,0:T(8,128)(2,1)S(1)}, bf16[960,1024]{1,0:T(8,128)(2,1)}) custom-call(bf16[192,4096]{1,0:T(8,128)(2,1)S(1)} %copy-done, bf16[192,4096]{1,0:T(8,128)(2,1)S(1)} %copy-done.1, bf16[960,2048]{1,0:T(8,128)(2,1)} %copy-done.2, bf16[960,2048]{1,0:T(8,128)(2,1)} %copy-done.2, ...), custom_call_target="tpu_custom_call" | custom-call | tf_op jit(solution)/shard_map/pallas_call | solution.py:95
  78.4 0.2 slice_bitcast_fusion.11
  78.6 1.4 copy-done.3
  80.0 0.2 slice_bitcast_fusion.10
  80.2 0.1 pad_maximum_fusion
  80.3 1.3 collective-permute-start.4
  81.6 0.1 pad_maximum_fusion.1
  81.7 1.3 collective-permute-start.5
  83.0 0.1 pad_maximum_fusion.2
  83.0 1.3 collective-permute-start.6
  84.3 0.1 pad_maximum_fusion.3
  84.4 1.3 collective-permute-start.7
  85.7 1.8 %collective-permute-done.4 = bf16[2,192,1024]{2,1,0:T(8,128)(2,1)S(1)} collective-permute-done((bf16[2,192,1024]{2,1,0:T(8,128)(2,1)S(1)}, bf16[2,192,1024]{2,1,0:T(8,128)(2,1)S(1)}, u32[]{:S(2)}, u32[]{:S(2)}) %collective-permute-start.4) | collective-permute-done | bytes 786464 | tf_op jit(solution)/shard_map/ppermute | solution.py:77
  87.5 40.5 %collective-permute-done.5 = bf16[2,192,1024]{2,1,0:T(8,128)(2,1)S(1)} collective-permute-done((bf16[2,192,1024]{2,1,0:T(8,128)(2,1)S(1)}, bf16[2,192,1024]{2,1,0:T(8,128)(2,1)S(1)}, u32[]{:S(2)}, u32[]{:S(2)}) %collective-permute-start.5) | collective-permute-done | bytes 786464 | tf_op jit(solution)/shard_map/ppermute | solution.py:77
  128.0 8.7 %collective-permute-done.6 = bf16[2,192,1024]{2,1,0:T(8,128)(2,1)S(1)} collective-permute-done((bf16[2,192,1024]{2,1,0:T(8,128)(2,1)S(1)}, bf16[2,192,1024]{2,1,0:T(8,128)(2,1)S(1)}, u32[]{:S(2)}, u32[]{:S(2)}) %collective-permute-start.6) | collective-permute-done | bytes 786464 | tf_op jit(solution)/shard_map/ppermute | solution.py:77
  136.7 34.3 %collective-permute-done.7 = bf16[2,192,1024]{2,1,0:T(8,128)(2,1)S(1)} collective-permute-done((bf16[2,192,1024]{2,1,0:T(8,128)(2,1)S(1)}, bf16[2,192,1024]{2,1,0:T(8,128)(2,1)S(1)}, u32[]{:S(2)}, u32[]{:S(2)}) %collective-permute-start.7) | collective-permute-done | bytes 786464 | tf_op jit(solution)/shard_map/ppermute | solution.py:77
  171.0 0.8 add_convert_fusion
  171.8 0.9 slice_bitcast_fusion
  (17 shorter events, 0.2 us)
Async XLA Ops:
  2.4 41.1 %copy-start.4 = (bf16[192,1024]{1,0:T(8,128)(2,1)S(1)}, bf16[192,1024]{1,0:T(8,128)(2,1)}, u32[]{:S(2)}) copy-start(bf16[192,1024]{1,0:T(8,128)(2,1)} %param.7) | copy-start | bytes 1179652
  4.2 23.2 %collective-permute-start = (bf16[192,2048]{1,0:T(8,128)(2,1)}, bf16[192,2048]{1,0:T(8,128)(2,1)S(1)}, u32[]{:S(2)}, u32[]{:S(2)}) collective-permute-start(bf16[192,2048]{1,0:T(8,128)(2,1)} %constant_dynamic-update-slice_fusion), channel_id=1, source_target_pairs={{0,4},{1,5},{2,6},{3,7},{4,8},{5,9},{6,10},{7,11},{8,12},{9,13},{1... | collective-permute-start | bytes 2359304 | tf_op jit(solution)/shard_map/ppermute | solution.py:77
  9.2 18.3 %collective-permute-start.1 = (bf16[192,2048]{1,0:T(8,128)(2,1)}, bf16[192,2048]{1,0:T(8,128)(2,1)S(1)}, u32[]{:S(2)}, u32[]{:S(2)}) collective-permute-start(bf16[192,2048]{1,0:T(8,128)(2,1)} %constant_dynamic-update-slice_fusion), channel_id=1, source_target_pairs={{0,3},{1,4},{2,5},{3,6},{4,7},{5,8},{6,9},{7,10},{8,11},{9,12},{10... | collective-permute-start | bytes 2359304 | tf_op jit(solution)/shard_map/ppermute | solution.py:77
  11.8 31.5 %collective-permute-start.2 = (bf16[192,2048]{1,0:T(8,128)(2,1)}, bf16[192,2048]{1,0:T(8,128)(2,1)S(1)}, u32[]{:S(2)}, u32[]{:S(2)}) collective-permute-start(bf16[192,2048]{1,0:T(8,128)(2,1)} %constant_dynamic-update-slice_fusion), channel_id=1, source_target_pairs={{0,2},{1,3},{2,4},{3,5},{4,6},{5,7},{6,8},{7,9},{8,10},{9,11},{10,... | collective-permute-start | bytes 2359304 | tf_op jit(solution)/shard_map/ppermute | solution.py:77
  15.3 28.2 %collective-permute-start.3 = (bf16[192,2048]{1,0:T(8,128)(2,1)}, bf16[192,2048]{1,0:T(8,128)(2,1)S(1)}, u32[]{:S(2)}, u32[]{:S(2)}) collective-permute-start(bf16[192,2048]{1,0:T(8,128)(2,1)} %constant_dynamic-update-slice_fusion), channel_id=1, source_target_pairs={{0,1},{1,2},{2,3},{3,4},{4,5},{5,6},{6,7},{7,8},{8,9},{9,10},{10,1... | collective-permute-start | bytes 2359304 | tf_op jit(solution)/shard_map/ppermute | solution.py:77
  20.3 23.3 %copy-start.5 = (bf16[192,1024]{1,0:T(8,128)(2,1)S(1)}, bf16[192,1024]{1,0:T(8,128)(2,1)}, u32[]{:S(2)}) copy-start(bf16[192,1024]{1,0:T(8,128)(2,1)} %param.8) | copy-start | bytes 1179652
  20.6 24.9 %copy-start = (bf16[192,4096]{1,0:T(8,128)(2,1)S(1)}, bf16[192,4096]{1,0:T(8,128)(2,1)}, u32[]{:S(2)}) copy-start(bf16[192,4096]{1,0:T(8,128)(2,1)} %q_ref.1) | copy-start | bytes 4718596
  20.6 24.8 %copy-start.1 = (bf16[192,4096]{1,0:T(8,128)(2,1)S(1)}, bf16[192,4096]{1,0:T(8,128)(2,1)}, u32[]{:S(2)}) copy-start(bf16[192,4096]{1,0:T(8,128)(2,1)} %do_ref.1) | copy-start | bytes 4718596
  43.6 1.9 %copy-start.2 = (bf16[960,2048]{1,0:T(8,128)(2,1)}, bf16[960,2048]{1,0:T(8,128)(2,1)S(1)}, u32[]{:S(2)}) copy-start(bf16[960,2048]{1,0:T(8,128)(2,1)S(1)} %constant_dynamic-update-slice_fusion.7.k_ref.v_ref) | copy-start | bytes 11796484
  78.4 1.5 copy-start.3
  80.3 7.2 %collective-permute-start.4 = (bf16[2,192,1024]{2,1,0:T(8,128)(2,1)S(1)}, bf16[2,192,1024]{2,1,0:T(8,128)(2,1)S(1)}, u32[]{:S(2)}, u32[]{:S(2)}) collective-permute-start(bf16[2,192,1024]{2,1,0:T(8,128)(2,1)S(1)} %pad_maximum_fusion), channel_id=1, source_target_pairs={{1,0},{2,1},{3,2},{4,3},{5,4},{6,5},{7,6},{8,7},{9,8},{10,9},{11,1... | collective-permute-start | bytes 2359304 | tf_op jit(solution)/shard_map/ppermute | solution.py:77
  81.7 46.3 %collective-permute-start.5 = (bf16[2,192,1024]{2,1,0:T(8,128)(2,1)S(1)}, bf16[2,192,1024]{2,1,0:T(8,128)(2,1)S(1)}, u32[]{:S(2)}, u32[]{:S(2)}) collective-permute-start(bf16[2,192,1024]{2,1,0:T(8,128)(2,1)S(1)} %pad_maximum_fusion.1), channel_id=1, source_target_pairs={{2,0},{3,1},{4,2},{5,3},{6,4},{7,5},{8,6},{9,7},{10,8},{11,9},{12,... | collective-permute-start | bytes 2359304 | tf_op jit(solution)/shard_map/ppermute | solution.py:77
  83.0 53.6 %collective-permute-start.6 = (bf16[2,192,1024]{2,1,0:T(8,128)(2,1)S(1)}, bf16[2,192,1024]{2,1,0:T(8,128)(2,1)S(1)}, u32[]{:S(2)}, u32[]{:S(2)}) collective-permute-start(bf16[2,192,1024]{2,1,0:T(8,128)(2,1)S(1)} %pad_maximum_fusion.2), channel_id=1, source_target_pairs={{3,0},{4,1},{5,2},{6,3},{7,4},{8,5},{9,6},{10,7},{11,8},{12,9},{13... | collective-permute-start | bytes 2359304 | tf_op jit(solution)/shard_map/ppermute | solution.py:77
  84.4 86.5 %collective-permute-start.7 = (bf16[2,192,1024]{2,1,0:T(8,128)(2,1)S(1)}, bf16[2,192,1024]{2,1,0:T(8,128)(2,1)S(1)}, u32[]{:S(2)}, u32[]{:S(2)}) collective-permute-start(bf16[2,192,1024]{2,1,0:T(8,128)(2,1)S(1)} %pad_maximum_fusion.3), channel_id=1, source_target_pairs={{4,0},{5,1},{6,2},{7,3},{8,4},{9,5},{10,6},{11,7},{12,8},{13,9},{1... | collective-permute-start | bytes 2359304 | tf_op jit(solution)/shard_map/ppermute | solution.py:77
where the time goes:
time: 173 us
  waiting for transfers between devices  108 us (62%)
  Pallas kernels  33 us (19%)
  starting transfers between devices  18.8 us (11%)
  local copies, waits for them, and re-layouts  10.7 us (6%)
    ppermute x8, waiting for transfers between devices, shift(): return lax.ppermute(x, 'ctx', route)  108 us
    pallas_call x1, Pallas kernels, per_device(): pl.pallas_call(kernel, grid=(HK,), in_specs=[pl.BlockSpec((tok, GROUP * D...  33 us
    ppermute x8, starting transfers between devices, shift(): return lax.ppermute(x, 'ctx', route)  18.8 us
    unnamed x18, local copies, waits for them, and re-layouts  5.24 us
  transfers between devices with their start and end apart: 8, of which 6 were waited for; matrix products, arithmetic and copies ran while one was open for 2% of the time, Pallas kernels for 0%

commit v1 on v0

v1 whole, which is shorter than its diff:
```python
import functools

import jax
import jax.numpy as jnp
from jax import lax
from jax.experimental import pallas as pl
from jax.experimental.pallas import tpu as pltpu
from jax.sharding import PartitionSpec as P

HQ = 32
HK = 8
DH = 128
GROUP = HQ // HK
WINDOW = 768
HALO = 4
SCALE = float(DH) ** (-0.5)
LOG2E = 1.4426950408889634
NEG = -1e30
SHIFT = 1 << 20
CHUNK = 256
NT = (((1,), (1,)), ((), ()))
TN = (((0,), (0,)), ((), ()))
NN = (((1,), (0,)), ((), ()))


def dot(a, b, dims):
    return lax.dot_general(a, b, dims, preferred_element_type=jnp.float32)


def tile_grads(k, v, q, do, bias):
    s = dot(k, q, NT) + bias
    dp = dot(v, do, NT)
    m = jnp.max(s, axis=0, keepdims=True)
    e = jnp.exp2((s - m) * (SCALE * LOG2E))
    inv = 1.0 / jnp.sum(e, axis=0, keepdims=True)
    delta = jnp.sum(e * dp, axis=0, keepdims=True) * inv
    p = (e * inv).astype(jnp.bfloat16)
    a = inv * SCALE
    ds = (e * (dp * a - delta * a)).astype(jnp.bfloat16)
    dv = dot(p, do, NN)
    dk = dot(ds, q, NN)
    dq = dot(ds, k, TN)
    return dq, dk, dv


def remote(src, dst, send, recv, device):
    return pltpu.make_async_remote_copy(
        src_ref=src,
        dst_ref=dst,
        send_sem=send,
        recv_sem=recv,
        device_id={"ctx": device},
        device_id_type=pl.DeviceIdType.MESH,
    )


def kernel(
    n, q_in, do_in, k_in, v_in, code_ref,
    dq_out, dk_out, dv_out,
    qd, kv, dqb, part, back, peer, acc_k, acc_v, bias,
    loc_sem, qd_send, qd_recv, kv_send, kv_recv, dq_sem, ret_send, ret_recv, peer_recv,
):
    tok = q_in.shape[0]
    heads = HK // 2
    wide = GROUP * DH
    span = (HALO + 1) * tok
    me = lax.axis_index("ctx")
    core = lax.rem(me, 2)
    chip = me // 2
    chips = n // 2
    mate = me + 1 - 2 * core
    other = 1 - core
    sides = (-2, -1, 1, 2)

    def dev(delta, c):
        return (chip + delta) * 2 + c

    def have(delta):
        return (chip + delta >= 0) & (chip + delta < chips)

    def cols(base, j, width):
        return pl.ds(pl.multiple_of((base * heads + j) * width, width), width)

    def rows(block):
        return pl.ds(pl.multiple_of(block * tok, 64), tok)

    barrier = pltpu.get_barrier_semaphore()
    pl.semaphore_signal(barrier, inc=1, device_id={"ctx": mate}, device_id_type=pl.DeviceIdType.MESH)
    for delta in sides:
        @pl.when(have(delta))
        def _(delta=delta):
            for c in range(2):
                pl.semaphore_signal(
                    barrier, inc=1, device_id={"ctx": dev(delta, c)}, device_id_type=pl.DeviceIdType.MESH
                )
    amount = 1 + 2 * (jnp.minimum(chip, 2) + jnp.minimum(chips - 1 - chip, 2))
    pl.semaphore_wait(barrier, amount)

    srcs = ((q_in, do_in), (k_in, v_in))

    def local_copies(j):
        out = []
        for a in range(2):
            out.append(pltpu.make_async_copy(
                srcs[0][a].at[:, cols(core, j, wide)], qd.at[j, a, core], loc_sem.at[j, a]))
            out.append(pltpu.make_async_copy(
                srcs[1][a].at[:, cols(core, j, DH)], kv.at[j, a, rows(HALO + core)], loc_sem.at[j, 2 + a]))
        return out

    def q_copy(j, a):
        return remote(srcs[0][a].at[:, cols(other, j, wide)], qd.at[j, a, core],
                      qd_send.at[j, a], qd_recv.at[j, a], mate)

    def q_arrival(j, a):
        return remote(srcs[0][a].at[:, cols(other, j, wide)], qd.at[j, a, other],
                      qd_send.at[j, a], qd_recv.at[j, a], mate)

    def kv_copy(j, a, delta, c):
        return remote(srcs[1][a].at[:, cols(c, j, DH)], kv.at[j, a, rows(HALO - 2 * delta + core)],
                      kv_send.at[j, a, 2 * delta + c], kv_recv.at[j, a, HALO - 2 * delta + core], dev(delta, c))

    def kv_arrival(j, a, block, c):
        return remote(srcs[1][a].at[:, cols(core, j, DH)], kv.at[j, a, rows(block)],
                      kv_send.at[j, a, 0], kv_recv.at[j, a, block], mate)

    @pl.loop(0, heads)
    def _(j):
        for delta in (2, 1):
            @pl.when(have(delta))
            def _(delta=delta):
                for c in range(2):
                    for a in range(2):
                        kv_copy(j, a, delta, c).start()
        for a in range(2):
            kv_copy(j, a, 0, other).start()
            q_copy(j, a).start()
        for copy in local_copies(j):
            copy.start()

    for delta in (1, 2):
        @pl.when(jnp.logical_not(have(-delta)))
        def _(delta=delta):
            lo = (HALO - 2 * delta) * tok
            kv[:, :, lo:lo + 2 * tok, :] = jnp.zeros((heads, 2, 2 * tok, DH), kv.dtype)

        @pl.when(jnp.logical_not(have(delta)))
        def _(delta=delta):
            back[delta - 1] = jnp.zeros(back.shape[1:], back.dtype)

    start = pl.multiple_of(chip * (2 * tok), 128)
    code = code_ref[:, pl.ds(start, span + tok)]
    column = jnp.broadcast_to(code, (8, span + tok)).T[:, 0:1]
    for b in range(2):
        lo = (HALO + b) * tok
        row = jnp.concatenate([code[:, lo:lo + tok]] * GROUP, axis=1)
        gap = row - column[b * tok:b * tok + span]
        bias[b] = jnp.where((gap >= 0) & (gap < WINDOW), 0.0, NEG).astype(jnp.float32)

    def ret_copy(j, block):
        delta = HALO // 2 - block // 2
        return remote(part.at[j, :, block * tok:(block + 1) * tok], back.at[delta - 1, core, j],
                      ret_send.at[j, block], ret_recv.at[j, delta - 1, core], dev(-delta, block % 2))

    def ret_arrival(j, delta, c):
        return remote(part.at[j, :, 0:tok], back.at[delta - 1, c, j],
                      ret_send.at[j, 0], ret_recv.at[j, delta - 1, c], mate)

    def peer_copy(j):
        return remote(part.at[j, :, rows(HALO + other)], peer.at[j],
                      ret_send.at[j, HALO], peer_recv.at[j], mate)

    def dq_copy(j):
        return remote(dqb.at[j, other], dq_out.at[:, cols(core, j, wide)],
                      dq_sem.at[j, 0], dq_sem.at[j, 1], mate)

    def dq_arrival(j):
        return remote(dqb.at[j, other], dq_out.at[:, cols(other, j, wide)],
                      dq_sem.at[j, 0], dq_sem.at[j, 1], mate)

    def dq_keep(j):
        return pltpu.make_async_copy(dqb.at[j, core], dq_out.at[:, cols(core, j, wide)], dq_sem.at[j, 2])

    @pl.loop(0, heads)
    def _(j):
        for copy in local_copies(j):
            copy.wait()
        for a in range(2):
            q_arrival(j, a).wait_recv()
            kv_arrival(j, a, HALO + other, 0).wait_recv()
        for delta in (2, 1):
            @pl.when(have(-delta))
            def _(delta=delta):
                for c in range(2):
                    for a in range(2):
                        kv_arrival(j, a, HALO - 2 * delta + c, 0).wait_recv()
        for b in range(2):
            k = kv[j, 0, b * tok:b * tok + span]
            v = kv[j, 1, b * tok:b * tok + span]
            q = jnp.concatenate([qd[j, 0, b, :, g * DH:(g + 1) * DH] for g in range(GROUP)], axis=0)
            do = jnp.concatenate([qd[j, 1, b, :, g * DH:(g + 1) * DH] for g in range(GROUP)], axis=0)
            dqs = []
            dk = dv = None
            for c in range(GROUP * tok // CHUNK):
                cut = slice(c * CHUNK, (c + 1) * CHUNK)
                dq, dk1, dv1 = tile_grads(k, v, q[cut], do[cut], bias[b, :, cut])
                dqs.append(dq.astype(jnp.bfloat16))
                dk = dk1 if dk is None else dk + dk1
                dv = dv1 if dv is None else dv + dv1
            dq = jnp.concatenate(dqs, axis=0)
            for g in range(GROUP):
                dqb[j, b, :, g * DH:(g + 1) * DH] = dq[g * tok:(g + 1) * tok]
            if b == 0:
                acc_k[...] = dk
                acc_v[...] = dv
            else:
                for a, (acc, new) in enumerate(((acc_k, dk), (acc_v, dv))):
                    part[j, a, 0:tok] = acc[0:tok].astype(jnp.bfloat16)
                    part[j, a, tok:span] = (acc[tok:span] + new[0:span - tok]).astype(jnp.bfloat16)
                    part[j, a, span:span + tok] = new[span - tok:span].astype(jnp.bfloat16)
        for block in range(HALO):
            @pl.when(have(block // 2 - HALO // 2))
            def _(block=block):
                ret_copy(j, block).start()
        peer_copy(j).start()
        dq_copy(j).start()
        dq_keep(j).start()

    @pl.loop(0, heads)
    def _(j):
        for delta in (1, 2):
            @pl.when(have(delta))
            def _(delta=delta):
                for c in range(2):
                    ret_arrival(j, delta, c).wait_recv()
        remote(part.at[j, :, 0:tok], peer.at[j], ret_send.at[j, HALO], peer_recv.at[j], mate).wait_recv()
        for a, out in enumerate((dk_out, dv_out)):
            mine = part[j, a, rows(HALO + core)].astype(jnp.float32)
            mine = mine + back[0, core, j, a].astype(jnp.float32) + back[1, core, j, a].astype(jnp.float32)
            out[:, cols(core, j, DH)] = mine.astype(jnp.bfloat16)
            his = peer[j, a].astype(jnp.float32)
            his = his + back[0, other, j, a].astype(jnp.float32) + back[1, other, j, a].astype(jnp.float32)
            out[:, cols(other, j, DH)] = his.astype(jnp.bfloat16)

    @pl.loop(0, heads)
    def _(j):
        for delta in (2, 1):
            @pl.when(have(delta))
            def _(delta=delta):
                for c in range(2):
                    for a in range(2):
                        kv_copy(j, a, delta, c).wait_send()
        for a in range(2):
            kv_copy(j, a, 0, other).wait_send()
            q_copy(j, a).wait_send()
        for block in range(HALO):
            @pl.when(have(block // 2 - HALO // 2))
            def _(block=block):
                ret_copy(j, block).wait_send()
        peer_copy(j).wait_send()
        dq_copy(j).wait_send()
        dq_arrival(j).wait_recv()
        dq_keep(j).wait()


def per_device(queries, keys, values, grad_out, positions, segments):
    tok = queries.shape[0]
    n = lax.axis_size("ctx")
    heads = HK // 2
    wide = GROUP * DH
    span = (HALO + 1) * tok
    code = positions + segments * SHIFT
    code = jnp.concatenate([jnp.full((HALO * tok,), -(1 << 30), jnp.int32), code])[None, :]
    bf = jnp.bfloat16
    dma = pltpu.SemaphoreType.DMA
    anywhere = pl.BlockSpec(memory_space=pl.ANY)
    vmem = pl.BlockSpec(memory_space=pltpu.VMEM)
    return pl.pallas_call(
        functools.partial(kernel, n),
        in_specs=[anywhere] * 4 + [vmem],
        out_specs=[anywhere, vmem, vmem],
        out_shape=[
            jax.ShapeDtypeStruct(queries.shape, bf),
            jax.ShapeDtypeStruct(keys.shape, bf),
            jax.ShapeDtypeStruct(values.shape, bf),
        ],
        scratch_shapes=[
            pltpu.VMEM((heads, 2, 2, tok, wide), bf),
            pltpu.VMEM((heads, 2, span + tok, DH), bf),
            pltpu.VMEM((heads, 2, tok, wide), bf),
            pltpu.VMEM((heads, 2, span + tok, DH), bf),
            pltpu.VMEM((2, 2, heads, 2, tok, DH), bf),
            pltpu.VMEM((heads, 2, tok, DH), bf),
            pltpu.VMEM((span, DH), jnp.float32),
            pltpu.VMEM((span, DH), jnp.float32),
            pltpu.VMEM((2, span, GROUP * tok), jnp.float32),
            dma((heads, 4)),
            dma((heads, 2)),
            dma((heads, 2)),
            dma((heads, 2, HALO + 2)),
            dma((heads, 2, HALO + 2)),
            dma((heads, 3)),
            dma((heads, HALO + 1)),
            dma((heads, 2, 2)),
            dma((heads,)),
        ],
        compiler_params=pltpu.CompilerParams(
            vmem_limit_bytes=56 * 1024 * 1024, collective_id=0, has_side_effects=True
        ),
    )(queries, grad_out, keys, values, code)


def solution(mesh):
    rows = P(("groups", "ctx"), None)
    return jax.shard_map(
        per_device,
        mesh=mesh,
        in_specs=(rows, rows, rows, rows, P("groups"), P("groups")),
        out_specs=(rows, rows, rows),
        check_vma=False,
    )
```

time: 173 us -> 65.3 us (0.38)
  the two profiles are of different devices: /device:TPU:0 before, /device:TPU:21 now
where the time goes in v1:
time: 65.3 us; the launch traced here: 64.8 us
  Pallas kernels  58.6 us (90%)
  local copies, waits for them, and re-layouts  4.89 us (7%)
  other arithmetic  0.73 us (1%)
  between operations  0.66 us (1%)
    pallas_call x1, Pallas kernels, per_device(): pl.pallas_call(functools.partial(kernel, n), in_specs=[anywhere] * 4 + [v...  58.6 us
    unnamed x7, local copies, waits for them, and re-layouts  4.27 us

profile of v1, /device:TPU:21, one launch (start us, length us, event | category | flops | bytes accessed | tf_op | source)
XLA Modules:
  0.0 64.8 jit_solution(18341497398575712536)
XLA Ops:
  0.6 0.7 %multiply_add_fusion = s32[3072]{0:T(1024)S(1)} fusion(s32[3072]{0:T(1024)} %param.10, s32[3072]{0:T(1024)} %param.11), kind=kLoop, calls=%fused_computation | loop fusion | flops 6144 | bytes 36864 | tf_op jit(solution)/shard_map/add | solution.py:271
  1.4 0.6 broadcast_in_dim.4.code_ref
  2.0 58.6 %shard_map.85 = (bf16[192,4096]{1,0:T(8,128)(2,1)}, bf16[192,1024]{1,0:T(8,128)(2,1)}, bf16[192,1024]{1,0:T(8,128)(2,1)}) custom-call(bf16[192,4096]{1,0:T(8,128)(2,1)} %q_in.1, bf16[192,4096]{1,0:T(8,128)(2,1)} %do_in.1, bf16[192,1024]{1,0:T(8,128)(2,1)} %k_in.1, bf16[192,1024]{1,0:T(8,128)(2,1)} %v_in.1, s32[1,3840]{1,0:T(1,128)} %broadcast_in_dim.4.code_ref), custom_call_target="tpu_custom_call" | custom-call | tf_op jit(solution)/shard_map/pallas_call | solution.py:277
  60.6 0.0 copy-start.1
  60.6 0.0 copy-start
  60.6 2.8 %copy.12 = bf16[192,4096]{1,0:T(8,128)(2,1)} copy(bf16[192,4096]{1,0:T(8,128)(2,1)} %get-tuple-element.6) | data formatting | bytes 3145728
  63.4 0.0 copy-done.1
  63.4 0.7 %copy.13 = bf16[192,1024]{1,0:T(8,128)(2,1)} copy(bf16[192,1024]{1,0:T(8,128)(2,1)S(1)} %copy-done.1) | data formatting | bytes 786432
  64.1 0.0 copy-done
  64.1 0.7 %copy.14 = bf16[192,1024]{1,0:T(8,128)(2,1)} copy(bf16[192,1024]{1,0:T(8,128)(2,1)S(1)} %copy-done) | data formatting | bytes 786432
  (1 shorter events, 0.0 us)
Async XLA Ops:
  60.6 2.8 %copy-start.1 = (bf16[192,1024]{1,0:T(8,128)(2,1)S(1)}, bf16[192,1024]{1,0:T(8,128)(2,1)}, u32[]{:S(2)}) copy-start(bf16[192,1024]{1,0:T(8,128)(2,1)} %get-tuple-element.7) | copy-start | bytes 1179652
  60.6 3.5 %copy-start = (bf16[192,1024]{1,0:T(8,128)(2,1)S(1)}, bf16[192,1024]{1,0:T(8,128)(2,1)}, u32[]{:S(2)}) copy-start(bf16[192,1024]{1,0:T(8,128)(2,1)} %get-tuple-element.8) | copy-start | bytes 1179652

commit v2 on v1

--- a/solution.py
+++ b/solution.py
@@ -212,12 +212,17 @@
             if b == 0:
                 acc_k[...] = dk
                 acc_v[...] = dv
+                part[j, 0, 0:tok] = dk[0:tok].astype(jnp.bfloat16)
+                part[j, 1, 0:tok] = dv[0:tok].astype(jnp.bfloat16)
+
+                @pl.when(have(-2))
+                def _():
+                    ret_copy(j, 0).start()
             else:
                 for a, (acc, new) in enumerate(((acc_k, dk), (acc_v, dv))):
-                    part[j, a, 0:tok] = acc[0:tok].astype(jnp.bfloat16)
                     part[j, a, tok:span] = (acc[tok:span] + new[0:span - tok]).astype(jnp.bfloat16)
                     part[j, a, span:span + tok] = new[span - tok:span].astype(jnp.bfloat16)
-        for block in range(HALO):
+        for block in range(1, HALO):
             @pl.when(have(block // 2 - HALO // 2))
             def _(block=block):
                 ret_copy(j, block).start()
@@ -262,6 +267,12 @@
         dq_keep(j).wait()
 
 
+def settle(*refs):
+    count = len(refs) // 2
+    for a in range(count):
+        refs[count + a][...] = refs[a][...]
+
+
 def per_device(queries, keys, values, grad_out, positions, segments):
     tok = queries.shape[0]
     n = lax.axis_size("ctx")
@@ -274,7 +285,7 @@
     dma = pltpu.SemaphoreType.DMA
     anywhere = pl.BlockSpec(memory_space=pl.ANY)
     vmem = pl.BlockSpec(memory_space=pltpu.VMEM)
-    return pl.pallas_call(
+    grads = pl.pallas_call(
         functools.partial(kernel, n),
         in_specs=[anywhere] * 4 + [vmem],
         out_specs=[anywhere, vmem, vmem],
@@ -307,6 +318,15 @@
             vmem_limit_bytes=56 * 1024 * 1024, collective_id=0, has_side_effects=True
         ),
     )(queries, grad_out, keys, values, code)
+    blocks = [pl.BlockSpec((tok // 4, g.shape[1]), lambda i: (i, 0)) for g in grads]
+    return pl.pallas_call(
+        settle,
+        grid=(4,),
+        in_specs=blocks,
+        out_specs=blocks,
+        out_shape=[jax.ShapeDtypeStruct(g.shape, g.dtype) for g in grads],
+        compiler_params=pltpu.CompilerParams(vmem_limit_bytes=60 * 1024 * 1024),
+    )(*grads)
 
 
 def solution(mesh):

time: 65.3 us -> 63 us (0.965)
  local copies, waits for them, and re-layouts: 4.89 us -> 0.62 us
  Pallas kernels: 58.6 us -> 60.6 us
    unnamed x7 -> x0, local copies, waits for them, and re-layouts: 4.27 us -> none
    pallas_call x0 -> x1, Pallas kernels: none -> 3.84 us  [per_device(): pl.pallas_call(settle, grid=(4,), in_specs=blocks, out_specs=blocks, out_...]
    pallas_call x1, Pallas kernels: 58.6 us -> 56.7 us  [per_device(): pl.pallas_call(functools.partial(kernel, n), in_specs=[anywhere] * 4 + [v...]
where the time goes in v2:
time: 63 us; the launch traced here: 62.6 us
  Pallas kernels  60.6 us (96%)
  other arithmetic  0.73 us (1%)
  between operations  0.64 us (1%)
    pallas_call x1, Pallas kernels, per_device(): pl.pallas_call(functools.partial(kernel, n), in_specs=[anywhere] * 4 + [v...  56.7 us
    pallas_call x1, Pallas kernels, per_device(): pl.pallas_call(settle, grid=(4,), in_specs=blocks, out_specs=blocks, out_...  3.84 us

profile of v2, /device:TPU:21, one launch (start us, length us, event | category | flops | bytes accessed | tf_op | source)
XLA Modules:
  0.0 62.6 jit_solution(11349151730542002559)
XLA Ops:
  0.6 0.7 %multiply_add_fusion = s32[3072]{0:T(1024)S(1)} fusion(s32[3072]{0:T(1024)} %param.10, s32[3072]{0:T(1024)} %param.11), kind=kLoop, calls=%fused_computation | loop fusion | flops 6144 | bytes 36864 | tf_op jit(solution)/shard_map/add | solution.py:282
  1.4 0.6 broadcast_in_dim.4.code_ref
  2.0 56.7 %shard_map.85 = (bf16[192,4096]{1,0:T(8,128)(2,1)}, bf16[192,1024]{1,0:T(8,128)(2,1)}, bf16[192,1024]{1,0:T(8,128)(2,1)}) custom-call(bf16[192,4096]{1,0:T(8,128)(2,1)} %q_in.1, bf16[192,4096]{1,0:T(8,128)(2,1)} %do_in.1, bf16[192,1024]{1,0:T(8,128)(2,1)} %k_in.1, bf16[192,1024]{1,0:T(8,128)(2,1)} %v_in.1, s32[1,3840]{1,0:T(1,128)} %broadcast_in_dim.4.code_ref), custom_call_target="tpu_custom_call" | custom-call | tf_op jit(solution)/shard_map/pallas_call | solution.py:288
  58.7 3.8 %shard_map.86 = (bf16[192,4096]{1,0:T(8,128)(2,1)}, bf16[192,1024]{1,0:T(8,128)(2,1)}, bf16[192,1024]{1,0:T(8,128)(2,1)}) custom-call(bf16[192,4096]{1,0:T(8,128)(2,1)} %get-tuple-element.6.refs_0_, bf16[192,1024]{1,0:T(8,128)(2,1)} %get-tuple-element.7.refs_1_, bf16[192,1024]{1,0:T(8,128)(2,1)} %get-tuple-element.8.refs_2_), custom_call_target="tpu_custom_call" | custom-call | tf_op jit(solution)/shard_map/pallas_call | solution.py:322
  (1 shorter events, 0.0 us)
